TPU v7x, 512 devices: a whole 4x8x8 slice. The times are simulated.
512 devices in a mesh: dp: 64 (over y, z), tensor: 8 (over x, core).
Axes of the slice: x: 4, y: 8, z: 8, core: 2. Of those that a mesh axis runs over, the one named last changes fastest.
Arguments:
- input_acts: bfloat16 [16384, 8192], P('dp', 'tensor'), may hold values from -6 to 6
- hidden_acts: bfloat16 [16384, 28672], P('dp', 'tensor'), may hold values from -6 to 6
- up_grads: bfloat16 [16384, 28672], P('dp', 'tensor'), may hold values from -144 to 144
- output_grads: bfloat16 [16384, 8192], P('dp', 'tensor'), may hold values from -144 to 144
- inner_up: bfloat16 [64, 8192], P(None, 'tensor'), may hold values from -0.0625 to 0.0625
- outer_up: bfloat16 [64, 28672], P(None, 'tensor'), may hold values from -0.09449112 to 0.09449112
- inner_down: bfloat16 [64, 28672], P(None, 'tensor'), may hold values from -0.03125 to 0.03125
- outer_down: bfloat16 [64, 8192], P(None, 'tensor'), may hold values from -0.176776695 to 0.176776695
Outputs:
- logged_up: float32 [256, 4096], P('dp', 'tensor')
- logged_down: float32 [256, 4096], P('dp', 'tensor')
- fisher_up: float32 [4096, 4096], P('dp', 'tensor')
- fisher_down: float32 [4096, 4096], P('dp', 'tensor')
All inputs are finite; a program needn't handle non-finite values.
Results may differ from a plain program's by a relative error of at most 0.0003.
Values sent between devices are 32-bit elements; how exact they have to be, the bound alone decides.
A program may use at most 64 MiB of HBM per device.

v0:
```python
import jax
import jax.numpy as jnp
from jax import lax
from jax.sharding import PartitionSpec as P

LEN = 64


DAMPING = 0.5


def project(acts, basis):
    return lax.dot_general(
        acts, basis, (((1,), (1,)), ((), ())), preferred_element_type=jnp.float32
    )


def contract_rows(left, right):
    return lax.dot_general(left, right, (((0,), (0,)), ((), ())), precision=lax.Precision.HIGHEST)


def per_sequence(grads, acts, seq_count):
    grad_width = grads.shape[1]
    act_width = acts.shape[1]
    grad_blocks = grads.reshape(seq_count, LEN, grad_width)
    act_blocks = acts.reshape(seq_count, LEN, act_width)
    outer = (
        jnp.einsum("slk,slm->skm", grad_blocks, act_blocks, precision=lax.Precision.HIGHEST) / LEN
    )
    return outer.reshape(seq_count, grad_width * act_width)


def body(
    input_acts, hidden_acts, up_grads, output_grads, inner_up, outer_up, inner_down, outer_down
):
    width = inner_up.shape[0]
    seq_count = input_acts.shape[0] // LEN
    flat_size = width * width
    col_count = flat_size // lax.axis_size("tensor")
    row_count = flat_size // lax.axis_size("dp")
    col_start = lax.axis_index("tensor") * col_count
    row_start = lax.axis_index("dp") * row_count
    total_seqs = seq_count * lax.axis_size("dp")
    partial_proj = jnp.concatenate(
        [
            project(input_acts, inner_up),
            project(up_grads, outer_up),
            project(hidden_acts, inner_down),
            project(output_grads, outer_down),
        ],
        axis=1,
    )
    summed = lax.psum(partial_proj, "tensor")
    local_up = per_sequence(summed[:, width : 2 * width], summed[:, :width], seq_count)
    local_down = per_sequence(summed[:, 3 * width :], summed[:, 2 * width : 3 * width], seq_count)
    cols_up = lax.dynamic_slice_in_dim(local_up, col_start, col_count, 1)
    cols_down = lax.dynamic_slice_in_dim(local_down, col_start, col_count, 1)
    row_ids = row_start + jnp.arange(row_count, dtype=jnp.int32)
    col_ids = col_start + jnp.arange(col_count, dtype=jnp.int32)
    diagonal_mask = (row_ids[:, None] == col_ids[None, :]).astype(jnp.float32)
    gathered_up, gathered_down = (
        lax.all_gather(local_up, "dp", axis=0, tiled=True),
        lax.all_gather(local_down, "dp", axis=0, tiled=True),
    )

    def slab(gathered):
        trace = jnp.sum(gathered * gathered) / total_seqs
        left_part = lax.dynamic_slice_in_dim(gathered, row_start, row_count, 1)
        right_part = lax.dynamic_slice_in_dim(gathered, col_start, col_count, 1)
        gram = contract_rows(left_part, right_part) / total_seqs
        return gram + DAMPING * trace / flat_size * diagonal_mask

    fisher_up = slab(gathered_up)
    fisher_down = slab(gathered_down)
    return (cols_up, cols_down, fisher_up, fisher_down)


def solution(mesh):
    in_specs = (
        P("dp", "tensor"),
        P("dp", "tensor"),
        P("dp", "tensor"),
        P("dp", "tensor"),
        P(None, "tensor"),
        P(None, "tensor"),
        P(None, "tensor"),
        P(None, "tensor"),
    )
    out_specs = (P("dp", "tensor"), P("dp", "tensor"), P("dp", "tensor"), P("dp", "tensor"))
    return jax.shard_map(body, mesh=mesh, in_specs=in_specs, out_specs=out_specs, check_vma=False)
```

profile of v0, /device:TPU:2, one launch (start us, length us, event | category | flops | bytes accessed | tf_op | source)
XLA Modules:
  0.0 288.9 jit_solution(5266898705545290835)
XLA Ops:
  7.2 0.0 all-reduce.2.cloned.1.call-start
  7.2 1.5 fusion.14
  8.7 0.1 copy-done
  8.9 1.7 fusion.13
  10.6 2.2 fusion.12
  12.8 0.3 fusion.11
  13.1 0.7 pad_maximum_fusion
  13.8 0.0 all-reduce.2.cloned.1.call-update
  13.9 0.0 all-gather.5.cloned.1.call-start
  13.9 73.1 %all-reduce.2.cloned.1.call-done = f32[256,256]{0,1:T(8,128)} async-done(((f32[256,256]{0,1:T(8,128)}), f32[256,256]{0,1:T(8,128)}) %all-reduce.2.cloned.1.call-update) | async-done | bytes 262160 | tf_op jit(solution)/shard_map/psum | solution.py:53
  87.0 1.0 fusion.10
  87.9 0.1 copy.20
  88.0 0.1 reshape.34
  88.1 0.3 convolution_multiply_fusion.3
  88.4 0.7 reshape.40
  89.1 0.0 all-gather.5.cloned.1.call-update
  89.2 0.0 all-gather.7.cloned.1.call-start
  89.2 0.1 copy.21
  89.3 0.1 reshape.37
  89.4 0.3 convolution_multiply_fusion.2
  89.7 0.7 reshape.42
  90.5 0.1 reshape.39
  90.6 0.1 reshape.36
  90.7 0.6 constant_dynamic-slice_fusion
  91.3 88.2 %all-gather.5.cloned.1.call-done = f32[64,4,4096]{2,1,0:T(4,128)} async-done(((f32[1,4,4096]{2,1,0:T(4,128)}), f32[64,4,4096]{2,1,0:T(4,128)}) %all-gather.5.cloned.1.call-update) | async-done | bytes 4194320 | tf_op jit(solution)/shard_map/all_gather | solution.py:62
  179.5 5.3 %reshape.41 = f32[256,4096]{1,0:T(8,128)} reshape(f32[64,4,4096]{2,1,0:T(4,128)} %all-gather.5.cloned.1.call-done) | data formatting | bytes 8388608
  184.8 3.9 %multiply_reduce_fusion.1 = f32[]{:T(128)} fusion(f32[256,4096]{1,0:T(8,128)} %reshape.41), kind=kLoop, calls=%fused_computation.1 | loop fusion | flops 2097151 | bytes 4194308 | tf_op jit(solution)/shard_map/reduce_sum | solution.py:67
  188.7 78.7 %all-gather.7.cloned.1.call-done = f32[64,4,4096]{2,1,0:T(4,128)} async-done(((f32[1,4,4096]{2,1,0:T(4,128)}), f32[64,4,4096]{2,1,0:T(4,128)}) %all-gather.7.cloned.1.call-update) | async-done | bytes 4194320 | tf_op jit(solution)/shard_map/all_gather | solution.py:63
  267.4 5.3 %reshape.43 = f32[256,4096]{1,0:T(8,128)} reshape(f32[64,4,4096]{2,1,0:T(4,128)} %all-gather.7.cloned.1.call-done) | data formatting | bytes 8388608
  272.7 3.9 %multiply_reduce_fusion = f32[]{:T(128)} fusion(f32[256,4096]{1,0:T(8,128)} %reshape.43), kind=kLoop, calls=%fused_computation | loop fusion | flops 2097151 | bytes 4194308 | tf_op jit(solution)/shard_map/reduce_sum | solution.py:67
  277.9 2.2 fusion.1
  280.1 2.2 fusion
  (8 shorter events, 0.0 us)
Async XLA Ops:
  7.2 1.7 copy-start
  7.2 5.6 %copy-start.1 = (bf16[256,1024]{1,0:T(8,128)(2,1)S(1)}, bf16[256,1024]{1,0:T(8,128)(2,1)}, u32[]{:S(2)}) copy-start(bf16[256,1024]{1,0:T(8,128)(2,1)} %param.8) | copy-start | bytes 1572868
  7.2 5.6 %copy-start.2 = (bf16[64,1024]{1,0:T(8,128)(2,1)S(1)}, bf16[64,1024]{1,0:T(8,128)(2,1)}, u32[]{:S(2)}) copy-start(bf16[64,1024]{1,0:T(8,128)(2,1)} %param.12) | copy-start | bytes 393220
  7.2 79.8 %all-reduce.2.cloned.1.call-start = ((), (), s32[]{:S(2)}) async-start(), calls=%async_computation | async-start | bytes 524288 | tf_op jit(solution)/shard_map/psum | solution.py:53
  13.9 165.6 %all-gather.5.cloned.1.call-start = ((), (), s32[]{:S(2)}) async-start(), calls=%async_computation.1 | async-start | bytes 4259840 | tf_op jit(solution)/shard_map/all_gather | solution.py:62
  89.2 178.3 %all-gather.7.cloned.1.call-start = ((), (), s32[]{:S(2)}) async-start(), calls=%async_computation.2 | async-start | bytes 4259840 | tf_op jit(solution)/shard_map/all_gather | solution.py:63
Sparse Core Ops, SparseCore 0:
  14.0 72.9 all-reduce.1
  91.0 88.4 all-gather.4
  183.5 83.8 all-gather.6
where the time goes:
time: 289 us
  waiting for transfers between devices  240 us (83%)
  between operations  15.2 us (5%)
  local copies, waits for them, and re-layouts  14.4 us (5%)
  matrix products  10.7 us (4%)
  other arithmetic  8.47 us (3%)
    all_gather x1, waiting for transfers between devices, body(): lax.all_gather(local_up, 'dp', axis=0, tiled=True)  88.2 us
    all_gather x1, waiting for transfers between devices, body(): lax.all_gather(local_down, 'dp', axis=0, tiled=True)  78.7 us
    psum x1, waiting for transfers between devices, body(): summed = lax.psum(partial_proj, 'tensor')  73.1 us
    unnamed x10, local copies, waits for them, and re-layouts  12.2 us
    reduce_sum x2, other arithmetic, slab(): trace = jnp.sum(gathered * gathered) / total_seqs  7.74 us
  transfers between devices with their start and end apart: 3, of which 3 were waited for; matrix products, arithmetic and copies ran while one was open for 4% of the time, Pallas kernels for 0%

commit v1 on v0

v1 whole, which is shorter than its diff:
```python
import functools

import jax
import jax.numpy as jnp
from jax import lax
from jax.experimental import pallas as pl
from jax.experimental.pallas import tpu as pltpu
from jax.sharding import PartitionSpec as P

LEN = 64
DAMPING = 0.5
WIDTH = 64
NT = 8
NY = 8
NZ = 8
SEQS = 256
FLAT = WIDTH * WIDTH
COLS = FLAT // NT
HALF = COLS // 2
LOADS = 4
MESH = pl.DeviceIdType.MESH
HIGHEST = lax.Precision.HIGHEST


def project(acts, basis):
    return lax.dot_general(
        acts, basis, (((1,), (1,)), ((), ())), preferred_element_type=jnp.float32
    )


def contract_rows(left, right):
    return lax.dot_general(
        left,
        right,
        (((0,), (0,)), ((), ())),
        precision=HIGHEST,
        preferred_element_type=jnp.float32,
    )


def kernel(
    ia, ha, ug, og, iu, ou, idn, od,
    log_up, log_dn, f_up, f_dn,
    x_ia, x_ha, x_ug, x_og, w_iu, w_ou, w_id, w_od,
    part, rs, mpad, a2a, ly, lz, lbuf, lp, ra, rb,
    load_sem,
    rs_s, rs_r, a2a_s, a2a_r, ly_s, ly_r, lz_s, lz_r, lt_s, lt_r,
    p1a_s, p1a_r, p1b_s, p1b_r, p2_s, p2_r,
):
    t = lax.axis_index("tensor")
    r = lax.axis_index("dp")
    y = r // NZ
    z = r % NZ

    def at_t(d):
        return (t + d) % NT

    def at_y(d):
        return (y + d) % NY

    def at_z(d):
        return (z + d) % NZ

    def remote(src, dst, send, recv, dp, tensor):
        return pltpu.make_async_remote_copy(
            src_ref=src,
            dst_ref=dst,
            send_sem=send,
            recv_sem=recv,
            device_id=(dp, tensor),
            device_id_type=MESH,
        )

    barrier = pltpu.get_barrier_semaphore()
    for d in range(1, NT):
        pl.semaphore_signal(barrier, inc=1, device_id=(r, at_t(d)), device_id_type=MESH)
    for d in range(1, NY):
        pl.semaphore_signal(barrier, inc=1, device_id=(at_y(d) * NZ + z, t), device_id_type=MESH)
    for d in range(1, NZ):
        pl.semaphore_signal(barrier, inc=1, device_id=(y * NZ + at_z(d), t), device_id_type=MESH)

    wide = ug.shape[1]
    piece = wide // LOADS
    loads = []

    def load(src, dst):
        copy = pltpu.make_async_copy(src, dst, load_sem.at[len(loads)])
        copy.start()
        loads.append(copy)
        return copy

    def wide_loads(src, dst):
        return [
            load(src.at[:, pl.ds(c * piece, piece)], dst.at[:, pl.ds(c * piece, piece)])
            for c in range(LOADS)
        ]

    up_narrow = [load(iu, w_iu), load(ia, x_ia)]
    up_basis = load(ou, w_ou)
    up_wide = wide_loads(ug, x_ug)
    dn_narrow = [load(od, w_od), load(og, x_og)]
    dn_basis = load(idn, w_id)
    dn_wide = wide_loads(ha, x_ha)

    def projected(narrow, basis, wides, x_n, w_n, x_w, w_w):
        for copy in narrow:
            copy.wait()
        slim = project(x_n[...], w_n[...])
        basis.wait()
        total = None
        for c, copy in enumerate(wides):
            copy.wait()
            cut = slice(c * piece, (c + 1) * piece)
            term = project(x_w[:, cut], w_w[:, cut])
            total = term if total is None else total + term
        return slim, total

    def scatter(first):
        for m in range(first, first + NT // 2):

            @pl.when(t != m)
            def _():
                remote(part.at[m], rs.at[t], rs_s.at[m], rs_r.at[t], r, m).start()

    act, grad = projected(up_narrow, up_basis, up_wide, x_ia, w_iu, x_ug, w_ou)
    part[0 : NT // 2] = jnp.concatenate([act, grad], axis=1).reshape(NT // 2, LEN, 2 * WIDTH)
    pl.semaphore_wait(barrier, (NT - 1) + (NY - 1) + (NZ - 1))
    scatter(0)
    grad, act = projected(dn_narrow, dn_basis, dn_wide, x_og, w_od, x_ha, w_id)
    part[NT // 2 :] = jnp.concatenate([act, grad], axis=1).reshape(NT // 2, LEN, 2 * WIDTH)
    scatter(NT // 2)

    total = part[t]
    for d in range(1, NT):
        src = at_t(d)
        remote(rs.at[src], rs.at[src], rs_s.at[src], rs_r.at[src], r, src).wait_recv()
        total = total + rs[src]
    outer = contract_rows(total, total)[WIDTH:] * (1.0 / LEN)
    lanes = lax.broadcasted_iota(jnp.int32, (WIDTH, 2 * WIDTH), 1)
    squares = jnp.sum(outer * outer, axis=0, keepdims=True)
    squares = pltpu.roll(jnp.broadcast_to(squares, (8, 2 * WIDTH)), WIDTH, 1)
    squares = jnp.broadcast_to(squares[0:1], (WIDTH, 2 * WIDTH))
    mpad[...] = jnp.where(lanes < WIDTH, outer, squares)

    def rows8(i):
        return pl.ds(pl.multiple_of(i * 8, 8), 8)

    for d in range(1, NT):
        to = at_t(d)
        remote(
            mpad.at[rows8(to)], a2a.at[rows8(t)], a2a_s.at[d], a2a_r.at[t], r, to
        ).start()
    for d in range(1, NY):
        to = at_y(d)
        remote(
            mpad.at[rows8(to)], ly.at[rows8(y)], ly_s.at[d], ly_r.at[y], to * NZ + z, t
        ).start()
    a2a[rows8(t), :] = mpad[rows8(t), :]
    ly[rows8(y), :] = mpad[rows8(y), :]

    for d in range(1, NT):
        src = at_t(d)
        remote(
            a2a.at[rows8(src)], a2a.at[rows8(src)], a2a_s.at[d], a2a_r.at[src], r, src
        ).wait_recv()
    lane8 = lax.broadcasted_iota(jnp.int32, (8, 2 * WIDTH), 1)
    sub8 = lax.broadcasted_iota(jnp.int32, (8, 2 * WIDTH), 0)
    for k in range(4):
        even = a2a[pl.ds(2 * k, 8, stride=8), :]
        odd = a2a[pl.ds(2 * k + 1, 8, stride=8), :]
        tile = jnp.where(lane8 < WIDTH, even, pltpu.roll(odd, WIDTH, 1))
        log_up[:, k * 128 : (k + 1) * 128] = tile[0:4]
        log_dn[:, k * 128 : (k + 1) * 128] = tile[4:8]
        half = ra if k < 2 else rb
        half[z, y, :, (k % 2) * 128 : (k % 2 + 1) * 128] = tile

    for d in range(1, NZ):
        to = at_z(d)
        remote(
            ra.at[z, y], ra.at[z, y], p1a_s.at[d], p1a_r.at[z], y * NZ + to, t
        ).start()
        to = at_y(d)
        remote(
            rb.at[z, y], rb.at[z, y], p1b_s.at[d], p1b_r.at[y], to * NZ + z, t
        ).start()

    for d in range(1, NY):
        src = at_y(d)
        remote(
            ly.at[rows8(src)], ly.at[rows8(src)], ly_s.at[d], ly_r.at[src], src * NZ + z, t
        ).wait_recv()
    for i in range(NZ):
        lz[i] = ly[pl.ds(i, 8, stride=8), :]
    for d in range(1, NZ):
        to = at_z(d)
        slot = pl.ds(pl.multiple_of(t * 64 + z * 8, 8), 8)
        remote(lz.at[to], lbuf.at[slot], lz_s.at[d], lz_r.at[z], y * NZ + to, t).start()
    lbuf[pl.ds(pl.multiple_of(t * 64 + z * 8, 8), 8), :] = lz[z]

    def leg(h, way, step, c):
        sign = 1 if way == 0 else -1
        if h == 0:
            origin = at_y(-sign * step + NY)
            ref = ra.at[pl.ds(4 * c, 4), origin]
            dp = at_y(sign + NY) * NZ + z
        else:
            origin = at_z(-sign * step + NZ)
            ref = rb.at[origin, pl.ds(4 * c, 4)]
            dp = y * NZ + at_z(sign + NZ)
        index = ((h * 2 + way) * 4 + step) * 2 + c
        return remote(ref, ref, p2_s.at[index], p2_r.at[index], dp, t)

    def arrived(h, way, step, c):
        sign = 1 if way == 0 else -1
        if h == 0:
            origin = at_y(-sign * (step + 1) + NY)
            ref = ra.at[pl.ds(4 * c, 4), origin]
        else:
            origin = at_z(-sign * (step + 1) + NZ)
            ref = rb.at[origin, pl.ds(4 * c, 4)]
        index = ((h * 2 + way) * 4 + step) * 2 + c
        remote(ref, ref, p2_s.at[index], p2_r.at[index], r, t).wait_recv()

    def runs(way, step, c):
        return step < 3 or c == way

    for d in range(1, NZ):
        src = at_z(d)
        remote(
            ra.at[src, y], ra.at[src, y], p1a_s.at[d], p1a_r.at[src], r, t
        ).wait_recv()
        src = at_y(d)
        remote(
            rb.at[z, src], rb.at[z, src], p1b_s.at[d], p1b_r.at[src], r, t
        ).wait_recv()
    for c in range(2):
        for h in range(2):
            for way in range(2):
                leg(h, way, 0, c).start()

    for d in range(1, NZ):
        src = at_z(d)
        slot = pl.ds(pl.multiple_of(t * 64 + src * 8, 8), 8)
        remote(lbuf.at[slot], lbuf.at[slot], lz_s.at[d], lz_r.at[src], r, t).wait_recv()

    def rows64(i):
        return pl.ds(pl.multiple_of(i * 64, 64), 64)

    for d in range(1, NT):
        remote(
            lbuf.at[rows64(t)], lbuf.at[rows64(t)], lt_s.at[d], lt_r.at[t], r, at_t(d)
        ).start()

    for step in range(1, 4):
        for c in range(2):
            for h in range(2):
                for way in range(2):
                    arrived(h, way, step - 1, c)
                    if runs(way, step, c):
                        leg(h, way, step, c).start()

    for d in range(1, NT):
        src = at_t(d)
        remote(
            lbuf.at[rows64(src)], lbuf.at[rows64(src)], lt_s.at[d], lt_r.at[src], r, t
        ).wait_recv()
    tally = jnp.zeros((8, 2 * WIDTH), jnp.float32)
    for i in range(NY * NZ):
        tile = lbuf[pl.ds(i, 8, stride=64), :]
        tally = tally + tile
        low = jnp.where((sub8 < 4) & (lane8 < WIDTH), tile, 0.0)
        high = jnp.where((sub8 >= 4) & (lane8 >= WIDTH), pltpu.roll(tile, WIDTH, 1), 0.0)
        lp[i * 8 : (i + 1) * 8, :] = low + high
    tally = jnp.where(lane8 >= WIDTH, tally, 0.0)
    trace_up = jnp.sum(jnp.where(sub8 < 4, tally, 0.0)) / SEQS
    trace_dn = jnp.sum(jnp.where(sub8 >= 4, tally, 0.0)) / SEQS

    row_ids = r * WIDTH + lax.broadcasted_iota(jnp.int32, (WIDTH, HALF), 0)
    col_ids = t * COLS + lax.broadcasted_iota(jnp.int32, (WIDTH, HALF), 1)
    for h in range(2):
        for way in range(2):
            arrived(h, way, 3, way)
        half = ra if h == 0 else rb
        gram = contract_rows(lp[...], half[...].reshape(8 * NY * NZ, HALF)) * (1.0 / SEQS)
        same = row_ids == col_ids + h * HALF
        cut = slice(h * HALF, (h + 1) * HALF)
        f_up[:, cut] = gram[:WIDTH] + jnp.where(same, DAMPING * trace_up / FLAT, 0.0)
        f_dn[:, cut] = gram[WIDTH:] + jnp.where(same, DAMPING * trace_dn / FLAT, 0.0)

    for m in range(NT):

        @pl.when(t != m)
        def _():
            remote(part.at[m], rs.at[t], rs_s.at[m], rs_r.at[t], r, m).wait_send()

    for d in range(1, NT):
        to = at_t(d)
        remote(mpad.at[rows8(to)], a2a.at[rows8(t)], a2a_s.at[d], a2a_r.at[t], r, to).wait_send()
        to = at_y(d)
        remote(mpad.at[rows8(to)], ly.at[rows8(y)], ly_s.at[d], ly_r.at[y], r, t).wait_send()
        to = at_z(d)
        remote(lz.at[to], lbuf.at[rows8(z)], lz_s.at[d], lz_r.at[z], r, t).wait_send()
        remote(lbuf.at[rows64(t)], lbuf.at[rows64(t)], lt_s.at[d], lt_r.at[t], r, t).wait_send()
        remote(ra.at[z, y], ra.at[z, y], p1a_s.at[d], p1a_r.at[z], r, t).wait_send()
        remote(rb.at[z, y], rb.at[z, y], p1b_s.at[d], p1b_r.at[y], r, t).wait_send()
    for step in range(4):
        for c in range(2):
            for h in range(2):
                for way in range(2):
                    if runs(way, step, c):
                        leg(h, way, step, c).wait_send()


def body(
    input_acts, hidden_acts, up_grads, output_grads, inner_up, outer_up, inner_down, outer_down
):
    operands = (
        input_acts,
        hidden_acts,
        up_grads,
        output_grads,
        inner_up,
        outer_up,
        inner_down,
        outer_down,
    )
    f32 = jnp.float32
    dma = pltpu.SemaphoreType.DMA
    return pl.pallas_call(
        kernel,
        out_shape=(
            jax.ShapeDtypeStruct((NT // 2, COLS), f32),
            jax.ShapeDtypeStruct((NT // 2, COLS), f32),
            jax.ShapeDtypeStruct((WIDTH, COLS), f32),
            jax.ShapeDtypeStruct((WIDTH, COLS), f32),
        ),
        in_specs=[pl.BlockSpec(memory_space=pl.ANY)] * 8,
        out_specs=[pl.BlockSpec(memory_space=pltpu.VMEM)] * 4,
        scratch_shapes=[pltpu.VMEM(a.shape, a.dtype) for a in operands]
        + [
            pltpu.VMEM((NT, LEN, 2 * WIDTH), f32),
            pltpu.VMEM((NT, LEN, 2 * WIDTH), f32),
            pltpu.VMEM((WIDTH, 2 * WIDTH), f32),
            pltpu.VMEM((8 * NT, 2 * WIDTH), f32),
            pltpu.VMEM((8 * NY, 2 * WIDTH), f32),
            pltpu.VMEM((NZ, NY, 2 * WIDTH), f32),
            pltpu.VMEM((NT * NZ * NY, 2 * WIDTH), f32),
            pltpu.VMEM((NT * NZ * NY, 2 * WIDTH), f32),
            pltpu.VMEM((NZ, NY, 8, HALF), f32),
            pltpu.VMEM((NZ, NY, 8, HALF), f32),
            dma((6 + 2 * LOADS,)),
        ]
        + [dma((8,))] * 14
        + [dma((32,))] * 2,
        compiler_params=pltpu.CompilerParams(
            collective_id=0, has_side_effects=True, vmem_limit_bytes=63 * 1024 * 1024
        ),
        cost_estimate=pl.CostEstimate(
            flops=2 * 256 * 64 * 9216, bytes_accessed=6 * 1024 * 1024, transcendentals=0
        ),
    )(*operands)


def solution(mesh):
    split = P("dp", "tensor")
    basis = P(None, "tensor")
    return jax.shard_map(
        body,
        mesh=mesh,
        in_specs=(split,) * 4 + (basis,) * 4,
        out_specs=(split,) * 4,
        check_vma=False,
    )
```

time: 289 us -> 52.6 us (0.18)
  the two profiles are of different devices: /device:TPU:2 before, /device:TPU:56 now
where the time goes in v1:
time: 52.6 us; the launch traced here: 52.4 us
  Pallas kernels  46 us (87%)
  local copies, waits for them, and re-layouts  5.72 us (11%)
  between operations  0.64 us (1%)
    pallas_call x1, Pallas kernels, body(): pl.pallas_call(kernel, out_shape=(jax.ShapeDtypeStruct((NT // 2, COLS), f...  46 us
    unnamed x4, local copies, waits for them, and re-layouts  5.72 us

profile of v1, /device:TPU:56, one launch (start us, length us, event | category | flops | bytes accessed | tf_op | source)
XLA Modules:
  0.0 52.4 jit_solution(10880708766386377576)
XLA Ops:
  0.6 46.0 %shard_map.111 = (f32[4,512]{1,0:T(4,128)}, f32[4,512]{1,0:T(4,128)}, f32[64,512]{1,0:T(8,128)}, f32[64,512]{1,0:T(8,128)}) custom-call(bf16[256,1024]{1,0:T(8,128)(2,1)} %ia.1, bf16[256,3584]{1,0:T(8,128)(2,1)} %ha.1, bf16[256,3584]{1,0:T(8,128)(2,1)} %ug.1, bf16[256,1024]{1,0:T(8,128)(2,1)} %og.1, bf16[64,1024]{1,0:T(8,128)(2,1)} %iu.1, ...), custom_call_target="tpu_custom_call" | custom-call | flops 301989888 | bytes 6291456 | tf_op jit(solution)/shard_map/pallas_call | solution.py:329
  46.6 1.3 %copy.16 = f32[4,512]{1,0:T(4,128)} copy(f32[4,512]{1,0:T(4,128)} %get-tuple-element.8) | data formatting | bytes 16384
  47.9 1.3 %copy.17 = f32[4,512]{1,0:T(4,128)} copy(f32[4,512]{1,0:T(4,128)} %get-tuple-element.9) | data formatting | bytes 16384
  49.2 1.6 %copy.18 = f32[64,512]{1,0:T(8,128)} copy(f32[64,512]{1,0:T(8,128)} %get-tuple-element.10) | data formatting | bytes 262144
  50.8 1.6 %copy.19 = f32[64,512]{1,0:T(8,128)} copy(f32[64,512]{1,0:T(8,128)} %get-tuple-element.11) | data formatting | bytes 262144

commit v2 on v1

v2 whole, which is shorter than its diff:
```python
import jax
import jax.numpy as jnp
from jax import lax
from jax.experimental import pallas as pl
from jax.experimental.pallas import tpu as pltpu
from jax.sharding import PartitionSpec as P

LEN = 64
DAMPING = 0.5
WIDTH = 64
NT = 8
NY = 8
NZ = 8
SEQS = 256
FLAT = WIDTH * WIDTH
COLS = FLAT // NT
HALF = COLS // 2
LOADS = 4
MESH = pl.DeviceIdType.MESH


def project(acts, basis):
    return lax.dot_general(
        acts, basis, (((1,), (1,)), ((), ())), preferred_element_type=jnp.float32
    )


def contract_rows(left, right):
    def split(values):
        high = values.astype(jnp.bfloat16)
        return high, (values - high.astype(jnp.float32)).astype(jnp.bfloat16)

    def dot(a, b):
        return lax.dot_general(
            a, b, (((0,), (0,)), ((), ())), preferred_element_type=jnp.float32
        )

    left_high, left_low = split(left)
    right_high, right_low = split(right)
    cross = dot(left_high, right_low) + dot(left_low, right_high)
    return cross + dot(left_high, right_high)


def kernel(
    ia, ha, ug, og, iu, ou, idn, od,
    log_up, log_dn, f_up, f_dn,
    x_ia, x_ha, x_ug, x_og, w_iu, w_ou, w_id, w_od,
    part, rs, mpad, a2a, ly, lz, lbuf, lp, ra, rb,
    v_lu, v_ld, v_fu, v_fd,
    load_sem, out_sem,
    rs_s, rs_r, a2a_s, a2a_r, ly_s, ly_r, lz_s, lz_r, lt_s, lt_r,
    p1a_s, p1a_r, p1b_s, p1b_r, p2_s, p2_r,
):
    t = lax.axis_index("tensor")
    r = lax.axis_index("dp")
    y = r // NZ
    z = r % NZ

    def at_t(d):
        return (t + d) % NT

    def at_y(d):
        return (y + d) % NY

    def at_z(d):
        return (z + d) % NZ

    def remote(src, dst, send, recv, dp, tensor):
        return pltpu.make_async_remote_copy(
            src_ref=src,
            dst_ref=dst,
            send_sem=send,
            recv_sem=recv,
            device_id=(dp, tensor),
            device_id_type=MESH,
        )

    started = []

    def send(*copy_of):
        copy = remote(*copy_of)
        copy.start()
        started.append(copy)

    writes = []

    def write(src, dst):
        copy = pltpu.make_async_copy(src, dst, out_sem.at[len(writes)])
        copy.start()
        writes.append(copy)

    def finish():
        for m in range(NT):

            @pl.when(t != m)
            def _():
                remote(part.at[m], rs.at[t], rs_s.at[m], rs_r.at[t], r, m).wait_send()

        for copy in started:
            copy.wait_send()

    wide = ug.shape[1]
    piece = wide // LOADS
    loads = []

    def load(src, dst):
        copy = pltpu.make_async_copy(src, dst, load_sem.at[len(loads)])
        copy.start()
        loads.append(copy)
        return copy

    def wide_loads(src, dst):
        return [
            load(src.at[:, pl.ds(c * piece, piece)], dst.at[:, pl.ds(c * piece, piece)])
            for c in range(LOADS)
        ]

    up_narrow = [load(iu, w_iu), load(ia, x_ia)]
    up_basis = load(ou, w_ou)
    up_wide = wide_loads(ug, x_ug)

    barrier = pltpu.get_barrier_semaphore()
    for d in range(1, NT):
        pl.semaphore_signal(barrier, inc=1, device_id=(r, at_t(d)), device_id_type=MESH)
    for d in range(1, NY):
        pl.semaphore_signal(barrier, inc=1, device_id=(at_y(d) * NZ + z, t), device_id_type=MESH)
    for d in range(1, NZ):
        pl.semaphore_signal(barrier, inc=1, device_id=(y * NZ + at_z(d), t), device_id_type=MESH)

    def projected(narrow, basis, wides, x_n, w_n, x_w, w_w):
        for copy in narrow:
            copy.wait()
        slim = project(x_n[...], w_n[...])
        basis.wait()
        total = None
        for c, copy in enumerate(wides):
            copy.wait()
            cut = slice(c * piece, (c + 1) * piece)
            term = project(x_w[:, cut], w_w[:, cut])
            total = term if total is None else total + term
        return slim, total

    def scatter(first):
        for m in range(first, first + NT // 2):

            @pl.when(t != m)
            def _():
                remote(part.at[m], rs.at[t], rs_s.at[m], rs_r.at[t], r, m).start()

    for copy in up_narrow:
        copy.wait()
    dn_narrow = [load(od, w_od), load(og, x_og)]
    dn_basis = load(idn, w_id)
    dn_wide = wide_loads(ha, x_ha)
    act, grad = projected([], up_basis, up_wide, x_ia, w_iu, x_ug, w_ou)
    part[0 : NT // 2] = jnp.concatenate([act, grad], axis=1).reshape(NT // 2, LEN, 2 * WIDTH)
    pl.semaphore_wait(barrier, (NT - 1) + (NY - 1) + (NZ - 1))
    scatter(0)
    grad, act = projected(dn_narrow, dn_basis, dn_wide, x_og, w_od, x_ha, w_id)
    part[NT // 2 :] = jnp.concatenate([act, grad], axis=1).reshape(NT // 2, LEN, 2 * WIDTH)
    scatter(NT // 2)

    total = part[t]
    for d in range(1, NT):
        src = at_t(d)
        remote(rs.at[src], rs.at[src], rs_s.at[src], rs_r.at[src], r, src).wait_recv()
        total = total + rs[src]
    outer = contract_rows(total, total)[WIDTH:] * (1.0 / LEN)
    lanes = lax.broadcasted_iota(jnp.int32, (WIDTH, 2 * WIDTH), 1)
    squares = jnp.sum(outer * outer, axis=0, keepdims=True)
    squares = pltpu.roll(jnp.broadcast_to(squares, (8, 2 * WIDTH)), WIDTH, 1)
    squares = jnp.broadcast_to(squares[0:1], (WIDTH, 2 * WIDTH))
    mpad[...] = jnp.where(lanes < WIDTH, outer, squares)

    def rows8(i):
        return pl.ds(pl.multiple_of(i * 8, 8), 8)

    for d in range(1, NT):
        to = at_t(d)
        send(
            mpad.at[rows8(to)], a2a.at[rows8(t)], a2a_s.at[d], a2a_r.at[t], r, to
        )
    for d in range(1, NY):
        to = at_y(d)
        send(
            mpad.at[rows8(to)], ly.at[rows8(y)], ly_s.at[d], ly_r.at[y], to * NZ + z, t
        )
    a2a[rows8(t), :] = mpad[rows8(t), :]
    ly[rows8(y), :] = mpad[rows8(y), :]

    for d in range(1, NT):
        src = at_t(d)
        remote(
            a2a.at[rows8(src)], a2a.at[rows8(src)], a2a_s.at[d], a2a_r.at[src], r, src
        ).wait_recv()
    lane8 = lax.broadcasted_iota(jnp.int32, (8, 2 * WIDTH), 1)
    sub8 = lax.broadcasted_iota(jnp.int32, (8, 2 * WIDTH), 0)
    for k in range(4):
        even = a2a[pl.ds(2 * k, 8, stride=8), :]
        odd = a2a[pl.ds(2 * k + 1, 8, stride=8), :]
        tile = jnp.where(lane8 < WIDTH, even, pltpu.roll(odd, WIDTH, 1))
        v_lu[:, k * 128 : (k + 1) * 128] = tile[0:4]
        v_ld[:, k * 128 : (k + 1) * 128] = tile[4:8]
        half = ra if k < 2 else rb
        half[z, y, :, (k % 2) * 128 : (k % 2 + 1) * 128] = tile

    for d in range(1, NZ):
        to = at_z(d)
        send(
            ra.at[z, y], ra.at[z, y], p1a_s.at[d], p1a_r.at[z], y * NZ + to, t
        )
        to = at_y(d)
        send(
            rb.at[z, y], rb.at[z, y], p1b_s.at[d], p1b_r.at[y], to * NZ + z, t
        )

    write(v_lu, log_up)
    write(v_ld, log_dn)

    for d in range(1, NY):
        src = at_y(d)
        remote(
            ly.at[rows8(src)], ly.at[rows8(src)], ly_s.at[d], ly_r.at[src], src * NZ + z, t
        ).wait_recv()
    for i in range(NZ):
        lz[i] = ly[pl.ds(i, 8, stride=8), :]
    for d in range(1, NZ):
        to = at_z(d)
        slot = pl.ds(pl.multiple_of(t * 64 + z * 8, 8), 8)
        send(lz.at[to], lbuf.at[slot], lz_s.at[d], lz_r.at[z], y * NZ + to, t)
    lbuf[pl.ds(pl.multiple_of(t * 64 + z * 8, 8), 8), :] = lz[z]

    def block(h, c, k):
        if h == 0:
            return ra.at[pl.ds(2 * c, 2), at_y(k + NY)]
        return rb.at[at_z(k + NZ), pl.ds(2 * c, 2)]

    def pass_on(h, c, k, shift, kind):
        ref = block(h, c, k)
        dp = at_y(shift + NY) * NZ + z if h == 0 else y * NZ + at_z(shift + NZ)
        seen = k - shift if k - shift > -4 else 4
        base = (h * 4 + c) * 8
        send(ref, ref, p2_s.at[base + kind], p2_r.at[base + seen + 3], dp, t)

    def arrived(h, c, k):
        ref = block(h, c, k)
        index = (h * 4 + c) * 8 + k + 3
        remote(ref, ref, p2_s.at[index], p2_r.at[index], r, t).wait_recv()

    for c in range(4):
        for h in range(2):
            for s in (2 * c, 2 * c + 1):

                @pl.when((z if h == 0 else y) != s)
                def _():
                    ref = ra.at[s, y] if h == 0 else rb.at[z, s]
                    sem = p1a_r if h == 0 else p1b_r
                    remote(ref, ref, p1a_s.at[0], sem.at[s], r, t).wait_recv()

            for kind, shift in enumerate((2, -2, 1, -1)):
                pass_on(h, c, 0, shift, kind)

    for d in range(1, NZ):
        src = at_z(d)
        slot = pl.ds(pl.multiple_of(t * 64 + src * 8, 8), 8)
        remote(lbuf.at[slot], lbuf.at[slot], lz_s.at[d], lz_r.at[src], r, t).wait_recv()

    def rows64(i):
        return pl.ds(pl.multiple_of(i * 64, 64), 64)

    for d in range(1, NT):
        send(lbuf.at[rows64(t)], lbuf.at[rows64(t)], lt_s.at[d], lt_r.at[t], r, at_t(d))

    for c in range(4):
        for h in range(2):
            arrived(h, c, -2)
            if c % 2 == 0:
                pass_on(h, c, -2, 2, 6)
            pass_on(h, c, -2, 1, 4)
            arrived(h, c, 2)
            if c % 2 == 1:
                pass_on(h, c, 2, -2, 6)
            pass_on(h, c, 2, -1, 5)

    for d in range(1, NT):
        src = at_t(d)
        remote(
            lbuf.at[rows64(src)], lbuf.at[rows64(src)], lt_s.at[d], lt_r.at[src], r, t
        ).wait_recv()
    tally = jnp.zeros((8, 2 * WIDTH), jnp.float32)
    for i in range(NY * NZ):
        tile = lbuf[pl.ds(i, 8, stride=64), :]
        tally = tally + tile
        low = jnp.where((sub8 < 4) & (lane8 < WIDTH), tile, 0.0)
        high = jnp.where((sub8 >= 4) & (lane8 >= WIDTH), pltpu.roll(tile, WIDTH, 1), 0.0)
        lp[i * 8 : (i + 1) * 8, :] = low + high
    tally = jnp.where(lane8 >= WIDTH, tally, 0.0)
    trace_up = jnp.sum(jnp.where(sub8 < 4, tally, 0.0)) / SEQS
    trace_dn = jnp.sum(jnp.where(sub8 >= 4, tally, 0.0)) / SEQS

    row_ids = r * WIDTH + lax.broadcasted_iota(jnp.int32, (WIDTH, HALF), 0)
    col_ids = t * COLS + lax.broadcasted_iota(jnp.int32, (WIDTH, HALF), 1)
    for h in range(2):
        for c in range(4):
            for k in (-1, 1, -3, 3, 4):
                arrived(h, c, k)
        half = ra if h == 0 else rb
        gram = contract_rows(lp[...], half[...].reshape(8 * NY * NZ, HALF)) * (1.0 / SEQS)
        same = row_ids == col_ids + h * HALF
        cut = slice(h * HALF, (h + 1) * HALF)
        v_fu[:, cut] = gram[:WIDTH] + jnp.where(same, DAMPING * trace_up / FLAT, 0.0)
        v_fd[:, cut] = gram[WIDTH:] + jnp.where(same, DAMPING * trace_dn / FLAT, 0.0)
        write(v_fu.at[:, cut], f_up.at[:, cut])
        write(v_fd.at[:, cut], f_dn.at[:, cut])

    finish()
    for copy in writes:
        copy.wait()


def hand_over(*refs):
    given, taken, held = refs[0:4], refs[4:8], refs[8:12]
    sem_in, sem_out = refs[12:]
    order = (2, 3, 0, 1)
    ins = [pltpu.make_async_copy(given[i], held[i], sem_in.at[i]) for i in order]
    outs = [pltpu.make_async_copy(held[i], taken[i], sem_out.at[i]) for i in order]
    for copy in ins:
        copy.start()
    for copy, onward in zip(ins, outs, strict=True):
        copy.wait()
        onward.start()
    for onward in outs:
        onward.wait()


def body(
    input_acts, hidden_acts, up_grads, output_grads, inner_up, outer_up, inner_down, outer_down
):
    operands = (
        input_acts,
        hidden_acts,
        up_grads,
        output_grads,
        inner_up,
        outer_up,
        inner_down,
        outer_down,
    )
    f32 = jnp.float32
    dma = pltpu.SemaphoreType.DMA
    shapes = [(NT // 2, COLS)] * 2 + [(WIDTH, COLS)] * 2
    out_shape = [jax.ShapeDtypeStruct(shape, f32) for shape in shapes]
    results = pl.pallas_call(
        kernel,
        out_shape=out_shape,
        in_specs=[pl.BlockSpec(memory_space=pltpu.HBM)] * 8,
        out_specs=[pl.BlockSpec(memory_space=pltpu.HBM)] * 4,
        scratch_shapes=[pltpu.VMEM(a.shape, a.dtype) for a in operands]
        + [
            pltpu.VMEM((NT, LEN, 2 * WIDTH), f32),
            pltpu.VMEM((NT, LEN, 2 * WIDTH), f32),
            pltpu.VMEM((WIDTH, 2 * WIDTH), f32),
            pltpu.VMEM((8 * NT, 2 * WIDTH), f32),
            pltpu.VMEM((8 * NY, 2 * WIDTH), f32),
            pltpu.VMEM((NZ, NY, 2 * WIDTH), f32),
            pltpu.VMEM((NT * NZ * NY, 2 * WIDTH), f32),
            pltpu.VMEM((NT * NZ * NY, 2 * WIDTH), f32),
            pltpu.VMEM((NZ, NY, 8, HALF), f32),
            pltpu.VMEM((NZ, NY, 8, HALF), f32),
        ]
        + [pltpu.VMEM(shape, f32) for shape in shapes]
        + [dma((6 + 2 * LOADS,)), dma((6,))]
        + [dma((8,))] * 14
        + [dma((64,))] * 2,
        compiler_params=pltpu.CompilerParams(
            collective_id=0, has_side_effects=True, vmem_limit_bytes=63 * 1024 * 1024
        ),
        cost_estimate=pl.CostEstimate(
            flops=2 * 256 * 64 * 9216, bytes_accessed=6 * 1024 * 1024, transcendentals=0
        ),
    )(*operands)
    return pl.pallas_call(
        hand_over,
        out_shape=out_shape,
        in_specs=[pl.BlockSpec(memory_space=pltpu.HBM)] * 4,
        out_specs=[pl.BlockSpec(memory_space=pltpu.HBM)] * 4,
        scratch_shapes=[pltpu.VMEM(shape, f32) for shape in shapes] + [dma((4,))] * 2,
    )(*results)


def solution(mesh):
    split = P("dp", "tensor")
    basis = P(None, "tensor")
    return jax.shard_map(
        body,
        mesh=mesh,
        in_specs=(split,) * 4 + (basis,) * 4,
        out_specs=(split,) * 4,
        check_vma=False,
    )
```

time: 52.6 us -> 44.1 us (0.84)
  the two profiles are of different devices: /device:TPU:56 before, /device:TPU:16 now
where the time goes in v2:
time: 44.1 us; the launch traced here: 43.9 us
  Pallas kernels  43.3 us (98%)
  between operations  0.64 us (1%)
    pallas_call x1, Pallas kernels, body(): pl.pallas_call(kernel, out_shape=out_shape, in_specs=[pl.BlockSpec(memory...  41.6 us
    pallas_call x1, Pallas kernels, body(): pl.pallas_call(hand_over, out_shape=out_shape, in_specs=[pl.BlockSpec(mem...  1.7 us

profile of v2, /device:TPU:16, one launch (start us, length us, event | category | flops | bytes accessed | tf_op | source)
XLA Modules:
  0.0 43.9 jit_solution(1702826607355645027)
XLA Ops:
  0.6 41.6 %shard_map.111 = (f32[4,512]{1,0:T(4,128)}, f32[4,512]{1,0:T(4,128)}, f32[64,512]{1,0:T(8,128)}, f32[64,512]{1,0:T(8,128)}) custom-call(bf16[256,1024]{1,0:T(8,128)(2,1)} %ia.1, bf16[256,3584]{1,0:T(8,128)(2,1)} %ha.1, bf16[256,3584]{1,0:T(8,128)(2,1)} %ug.1, bf16[256,1024]{1,0:T(8,128)(2,1)} %og.1, bf16[64,1024]{1,0:T(8,128)(2,1)} %iu.1, ...), custom_call_target="tpu_custom_call" | custom-call | flops 301989888 | bytes 6291456 | tf_op jit(solution)/shard_map/pallas_call | solution.py:353
  42.2 1.7 %shard_map.112 = (f32[4,512]{1,0:T(4,128)}, f32[4,512]{1,0:T(4,128)}, f32[64,512]{1,0:T(8,128)}, f32[64,512]{1,0:T(8,128)}) custom-call(f32[4,512]{1,0:T(4,128)} %get-tuple-element.8.refs_0_, f32[4,512]{1,0:T(4,128)} %get-tuple-element.9.refs_1_, f32[64,512]{1,0:T(8,128)} %get-tuple-element.10.refs_2_, f32[64,512]{1,0:T(8,128)} %get-tuple-element.11.refs_3_), custom_call_target="tpu_custom_call" | custom-call | tf_op jit(solution)/shard_map/pallas_call | solution.py:382

commit v3 on v2

--- a/solution.py
+++ b/solution.py
@@ -15,7 +15,10 @@
 FLAT = WIDTH * WIDTH
 COLS = FLAT // NT
 HALF = COLS // 2
-LOADS = 4
+PIECES = 4
+SLOTS = 8 // PIECES
+CUTS = (0, 512, 1536, 3584)
+FAR_FIRST = (4, 3, 5, 2, 6, 1, 7)
 MESH = pl.DeviceIdType.MESH
 
 
@@ -25,20 +28,19 @@
     )
 
 
-def contract_rows(left, right):
-    def split(values):
-        high = values.astype(jnp.bfloat16)
-        return high, (values - high.astype(jnp.float32)).astype(jnp.bfloat16)
-
+def split(values):
+    high = values.astype(jnp.bfloat16)
+    return high, (values - high.astype(jnp.float32)).astype(jnp.bfloat16)
+
+
+def times(left, right):
     def dot(a, b):
         return lax.dot_general(
-            a, b, (((0,), (0,)), ((), ())), preferred_element_type=jnp.float32
-        )
-
-    left_high, left_low = split(left)
-    right_high, right_low = split(right)
-    cross = dot(left_high, right_low) + dot(left_low, right_high)
-    return cross + dot(left_high, right_high)
+            a, b, (((1,), (0,)), ((), ())), preferred_element_type=jnp.float32
+        )
+
+    cross = dot(left[0], right[1]) + dot(left[1], right[0])
+    return cross + dot(left[0], right[0])
 
 
 def kernel(
@@ -59,6 +61,13 @@
     def at_t(d):
         return (t + d) % NT
 
+    x = t // 2
+
+    def item_of(device):
+        return device % 2 * (NT // 2) + device // 2
+
+    item = item_of(t)
+
     def at_y(d):
         return (y + d) % NY
 
@@ -89,35 +98,10 @@
         copy.start()
         writes.append(copy)
 
-    def finish():
-        for m in range(NT):
-
-            @pl.when(t != m)
-            def _():
-                remote(part.at[m], rs.at[t], rs_s.at[m], rs_r.at[t], r, m).wait_send()
-
+    def settle():
         for copy in started:
             copy.wait_send()
-
-    wide = ug.shape[1]
-    piece = wide // LOADS
-    loads = []
-
-    def load(src, dst):
-        copy = pltpu.make_async_copy(src, dst, load_sem.at[len(loads)])
-        copy.start()
-        loads.append(copy)
-        return copy
-
-    def wide_loads(src, dst):
-        return [
-            load(src.at[:, pl.ds(c * piece, piece)], dst.at[:, pl.ds(c * piece, piece)])
-            for c in range(LOADS)
-        ]
-
-    up_narrow = [load(iu, w_iu), load(ia, x_ia)]
-    up_basis = load(ou, w_ou)
-    up_wide = wide_loads(ug, x_ug)
+        started.clear()
 
     barrier = pltpu.get_barrier_semaphore()
     for d in range(1, NT):
@@ -126,6 +110,27 @@
         pl.semaphore_signal(barrier, inc=1, device_id=(at_y(d) * NZ + z, t), device_id_type=MESH)
     for d in range(1, NZ):
         pl.semaphore_signal(barrier, inc=1, device_id=(y * NZ + at_z(d), t), device_id_type=MESH)
+
+    loads = []
+
+    def load(src, dst):
+        copy = pltpu.make_async_copy(src, dst, load_sem.at[len(loads)])
+        copy.start()
+        loads.append(copy)
+        return copy
+
+    def wide_loads(src, dst):
+        return [
+            load(src.at[:, pl.ds(a, b - a)], dst.at[:, pl.ds(a, b - a)])
+            for a, b in zip(CUTS[:-1], CUTS[1:], strict=True)
+        ]
+
+    up_narrow = [load(iu, w_iu), load(ia, x_ia)]
+    up_basis = load(ou, w_ou)
+    up_wide = wide_loads(ug, x_ug)
+    dn_narrow = [load(od, w_od), load(og, x_og)]
+    dn_basis = load(idn, w_id)
+    dn_wide = wide_loads(ha, x_ha)
 
     def projected(narrow, basis, wides, x_n, w_n, x_w, w_w):
         for copy in narrow:
@@ -135,37 +140,35 @@
         total = None
         for c, copy in enumerate(wides):
             copy.wait()
-            cut = slice(c * piece, (c + 1) * piece)
+            cut = slice(CUTS[c], CUTS[c + 1])
             term = project(x_w[:, cut], w_w[:, cut])
             total = term if total is None else total + term
         return slim, total
 
-    def scatter(first):
-        for m in range(first, first + NT // 2):
-
-            @pl.when(t != m)
+    def scatter(side):
+        for d in range(NT // 2):
+            other = (x + d) % (NT // 2)
+            m = side * (NT // 2) + other
+            to = 2 * other + side
+
+            @pl.when(t != to)
             def _():
-                remote(part.at[m], rs.at[t], rs_s.at[m], rs_r.at[t], r, m).start()
-
-    for copy in up_narrow:
-        copy.wait()
-    dn_narrow = [load(od, w_od), load(og, x_og)]
-    dn_basis = load(idn, w_id)
-    dn_wide = wide_loads(ha, x_ha)
-    act, grad = projected([], up_basis, up_wide, x_ia, w_iu, x_ug, w_ou)
+                remote(part.at[m], rs.at[t], rs_s.at[m], rs_r.at[t], r, to).start()
+
+    act, grad = projected(up_narrow, up_basis, up_wide, x_ia, w_iu, x_ug, w_ou)
     part[0 : NT // 2] = jnp.concatenate([act, grad], axis=1).reshape(NT // 2, LEN, 2 * WIDTH)
     pl.semaphore_wait(barrier, (NT - 1) + (NY - 1) + (NZ - 1))
     scatter(0)
     grad, act = projected(dn_narrow, dn_basis, dn_wide, x_og, w_od, x_ha, w_id)
     part[NT // 2 :] = jnp.concatenate([act, grad], axis=1).reshape(NT // 2, LEN, 2 * WIDTH)
-    scatter(NT // 2)
-
-    total = part[t]
+    scatter(1)
+
+    total = part[item]
     for d in range(1, NT):
         src = at_t(d)
         remote(rs.at[src], rs.at[src], rs_s.at[src], rs_r.at[src], r, src).wait_recv()
         total = total + rs[src]
-    outer = contract_rows(total, total)[WIDTH:] * (1.0 / LEN)
+    outer = times(split(total.T), split(total))[WIDTH:] * (1.0 / LEN)
     lanes = lax.broadcasted_iota(jnp.int32, (WIDTH, 2 * WIDTH), 1)
     squares = jnp.sum(outer * outer, axis=0, keepdims=True)
     squares = pltpu.roll(jnp.broadcast_to(squares, (8, 2 * WIDTH)), WIDTH, 1)
@@ -175,23 +178,23 @@
     def rows8(i):
         return pl.ds(pl.multiple_of(i * 8, 8), 8)
 
-    for d in range(1, NT):
+    for d in FAR_FIRST:
         to = at_t(d)
         send(
-            mpad.at[rows8(to)], a2a.at[rows8(t)], a2a_s.at[d], a2a_r.at[t], r, to
-        )
-    for d in range(1, NY):
+            mpad.at[rows8(to)], a2a.at[rows8(item)], a2a_s.at[d], a2a_r.at[t], r, to
+        )
+    for d in FAR_FIRST:
         to = at_y(d)
         send(
             mpad.at[rows8(to)], ly.at[rows8(y)], ly_s.at[d], ly_r.at[y], to * NZ + z, t
         )
-    a2a[rows8(t), :] = mpad[rows8(t), :]
+    a2a[rows8(item), :] = mpad[rows8(t), :]
     ly[rows8(y), :] = mpad[rows8(y), :]
 
     for d in range(1, NT):
         src = at_t(d)
         remote(
-            a2a.at[rows8(src)], a2a.at[rows8(src)], a2a_s.at[d], a2a_r.at[src], r, src
+            a2a.at[rows8(item_of(src))], a2a.at[rows8(item_of(src))], a2a_s.at[d], a2a_r.at[src], r, src
         ).wait_recv()
     lane8 = lax.broadcasted_iota(jnp.int32, (8, 2 * WIDTH), 1)
     sub8 = lax.broadcasted_iota(jnp.int32, (8, 2 * WIDTH), 0)
@@ -204,7 +207,7 @@
         half = ra if k < 2 else rb
         half[z, y, :, (k % 2) * 128 : (k % 2 + 1) * 128] = tile
 
-    for d in range(1, NZ):
+    for d in FAR_FIRST:
         to = at_z(d)
         send(
             ra.at[z, y], ra.at[z, y], p1a_s.at[d], p1a_r.at[z], y * NZ + to, t
@@ -224,32 +227,32 @@
         ).wait_recv()
     for i in range(NZ):
         lz[i] = ly[pl.ds(i, 8, stride=8), :]
-    for d in range(1, NZ):
+    for d in FAR_FIRST:
         to = at_z(d)
-        slot = pl.ds(pl.multiple_of(t * 64 + z * 8, 8), 8)
+        slot = pl.ds(pl.multiple_of(item * 64 + z * 8, 8), 8)
         send(lz.at[to], lbuf.at[slot], lz_s.at[d], lz_r.at[z], y * NZ + to, t)
-    lbuf[pl.ds(pl.multiple_of(t * 64 + z * 8, 8), 8), :] = lz[z]
+    lbuf[pl.ds(pl.multiple_of(item * 64 + z * 8, 8), 8), :] = lz[z]
 
     def block(h, c, k):
         if h == 0:
-            return ra.at[pl.ds(2 * c, 2), at_y(k + NY)]
-        return rb.at[at_z(k + NZ), pl.ds(2 * c, 2)]
+            return ra.at[pl.ds(SLOTS * c, SLOTS), at_y(k + NY)]
+        return rb.at[at_z(k + NZ), pl.ds(SLOTS * c, SLOTS)]
 
     def pass_on(h, c, k, shift, kind):
         ref = block(h, c, k)
         dp = at_y(shift + NY) * NZ + z if h == 0 else y * NZ + at_z(shift + NZ)
         seen = k - shift if k - shift > -4 else 4
-        base = (h * 4 + c) * 8
+        base = (h * PIECES + c) * 8
         send(ref, ref, p2_s.at[base + kind], p2_r.at[base + seen + 3], dp, t)
 
     def arrived(h, c, k):
         ref = block(h, c, k)
-        index = (h * 4 + c) * 8 + k + 3
+        index = (h * PIECES + c) * 8 + k + 3
         remote(ref, ref, p2_s.at[index], p2_r.at[index], r, t).wait_recv()
 
-    for c in range(4):
+    for c in range(PIECES):
         for h in range(2):
-            for s in (2 * c, 2 * c + 1):
+            for s in range(SLOTS * c, SLOTS * (c + 1)):
 
                 @pl.when((z if h == 0 else y) != s)
                 def _():
@@ -262,16 +265,16 @@
 
     for d in range(1, NZ):
         src = at_z(d)
-        slot = pl.ds(pl.multiple_of(t * 64 + src * 8, 8), 8)
+        slot = pl.ds(pl.multiple_of(item * 64 + src * 8, 8), 8)
         remote(lbuf.at[slot], lbuf.at[slot], lz_s.at[d], lz_r.at[src], r, t).wait_recv()
 
     def rows64(i):
         return pl.ds(pl.multiple_of(i * 64, 64), 64)
 
     for d in range(1, NT):
-        send(lbuf.at[rows64(t)], lbuf.at[rows64(t)], lt_s.at[d], lt_r.at[t], r, at_t(d))
-
-    for c in range(4):
+        send(lbuf.at[rows64(item)], lbuf.at[rows64(item)], lt_s.at[d], lt_r.at[t], r, at_t(d))
+
+    for c in range(PIECES):
         for h in range(2):
             arrived(h, c, -2)
             if c % 2 == 0:
@@ -282,10 +285,17 @@
                 pass_on(h, c, 2, -2, 6)
             pass_on(h, c, 2, -1, 5)
 
+    for m in range(NT):
+
+        @pl.when(item != m)
+        def _():
+            remote(part.at[m], rs.at[t], rs_s.at[m], rs_r.at[t], r, m).wait_send()
+
+    settle()
     for d in range(1, NT):
         src = at_t(d)
         remote(
-            lbuf.at[rows64(src)], lbuf.at[rows64(src)], lt_s.at[d], lt_r.at[src], r, t
+            lbuf.at[rows64(item_of(src))], lbuf.at[rows64(item_of(src))], lt_s.at[d], lt_r.at[src], r, t
         ).wait_recv()
     tally = jnp.zeros((8, 2 * WIDTH), jnp.float32)
     for i in range(NY * NZ):
@@ -298,14 +308,15 @@
     trace_up = jnp.sum(jnp.where(sub8 < 4, tally, 0.0)) / SEQS
     trace_dn = jnp.sum(jnp.where(sub8 >= 4, tally, 0.0)) / SEQS
 
+    left = split(lp[...].T)
     row_ids = r * WIDTH + lax.broadcasted_iota(jnp.int32, (WIDTH, HALF), 0)
     col_ids = t * COLS + lax.broadcasted_iota(jnp.int32, (WIDTH, HALF), 1)
     for h in range(2):
-        for c in range(4):
+        for c in range(PIECES):
             for k in (-1, 1, -3, 3, 4):
                 arrived(h, c, k)
         half = ra if h == 0 else rb
-        gram = contract_rows(lp[...], half[...].reshape(8 * NY * NZ, HALF)) * (1.0 / SEQS)
+        gram = times(left, split(half[...].reshape(8 * NY * NZ, HALF))) * (1.0 / SEQS)
         same = row_ids == col_ids + h * HALF
         cut = slice(h * HALF, (h + 1) * HALF)
         v_fu[:, cut] = gram[:WIDTH] + jnp.where(same, DAMPING * trace_up / FLAT, 0.0)
@@ -313,7 +324,7 @@
         write(v_fu.at[:, cut], f_up.at[:, cut])
         write(v_fd.at[:, cut], f_dn.at[:, cut])
 
-    finish()
+    settle()
     for copy in writes:
         copy.wait()
 
@@ -369,7 +380,7 @@
             pltpu.VMEM((NZ, NY, 8, HALF), f32),
         ]
         + [pltpu.VMEM(shape, f32) for shape in shapes]
-        + [dma((6 + 2 * LOADS,)), dma((6,))]
+        + [dma((6 + 2 * (len(CUTS) - 1),)), dma((6,))]
         + [dma((8,))] * 14
         + [dma((64,))] * 2,
         compiler_params=pltpu.CompilerParams(

time: 44.1 us -> 42.5 us (0.964)
  Pallas kernels: 43.3 us -> 41.7 us
    pallas_call x1, Pallas kernels: 41.6 us -> 40 us  [body(): pl.pallas_call(kernel, out_shape=out_shape, in_specs=[pl.BlockSpec(memory...]
where the time goes in v3:
time: 42.5 us; the launch traced here: 42.3 us
  Pallas kernels  41.7 us (98%)
  between operations  0.64 us (2%)
    pallas_call x1, Pallas kernels, body(): pl.pallas_call(kernel, out_shape=out_shape, in_specs=[pl.BlockSpec(memory...  40 us
    pallas_call x1, Pallas kernels, body(): pl.pallas_call(hand_over, out_shape=out_shape, in_specs=[pl.BlockSpec(mem...  1.7 us

profile of v3, /device:TPU:16, one launch (start us, length us, event | category | flops | bytes accessed | tf_op | source)
XLA Modules:
  0.0 42.3 jit_solution(2419374514730657564)
XLA Ops:
  0.6 40.0 %shard_map.111 = (f32[4,512]{1,0:T(4,128)}, f32[4,512]{1,0:T(4,128)}, f32[64,512]{1,0:T(8,128)}, f32[64,512]{1,0:T(8,128)}) custom-call(bf16[256,1024]{1,0:T(8,128)(2,1)} %ia.1, bf16[256,3584]{1,0:T(8,128)(2,1)} %ha.1, bf16[256,3584]{1,0:T(8,128)(2,1)} %ug.1, bf16[256,1024]{1,0:T(8,128)(2,1)} %og.1, bf16[64,1024]{1,0:T(8,128)(2,1)} %iu.1, ...), custom_call_target="tpu_custom_call" | custom-call | flops 301989888 | bytes 6291456 | tf_op jit(solution)/shard_map/pallas_call | solution.py:364
  40.6 1.7 %shard_map.112 = (f32[4,512]{1,0:T(4,128)}, f32[4,512]{1,0:T(4,128)}, f32[64,512]{1,0:T(8,128)}, f32[64,512]{1,0:T(8,128)}) custom-call(f32[4,512]{1,0:T(4,128)} %get-tuple-element.8.refs_0_, f32[4,512]{1,0:T(4,128)} %get-tuple-element.9.refs_1_, f32[64,512]{1,0:T(8,128)} %get-tuple-element.10.refs_2_, f32[64,512]{1,0:T(8,128)} %get-tuple-element.11.refs_3_), custom_call_target="tpu_custom_call" | custom-call | tf_op jit(solution)/shard_map/pallas_call | solution.py:393

commit v4 on v3

--- a/solution.py
+++ b/solution.py
@@ -45,11 +45,10 @@
 
 def kernel(
     ia, ha, ug, og, iu, ou, idn, od,
-    log_up, log_dn, f_up, f_dn,
+    v_lu, v_ld, v_fu, v_fd,
     x_ia, x_ha, x_ug, x_og, w_iu, w_ou, w_id, w_od,
     part, rs, mpad, a2a, ly, lz, lbuf, lp, ra, rb,
-    v_lu, v_ld, v_fu, v_fd,
-    load_sem, out_sem,
+    load_sem,
     rs_s, rs_r, a2a_s, a2a_r, ly_s, ly_r, lz_s, lz_r, lt_s, lt_r,
     p1a_s, p1a_r, p1b_s, p1b_r, p2_s, p2_r,
 ):
@@ -90,13 +89,6 @@
         copy = remote(*copy_of)
         copy.start()
         started.append(copy)
-
-    writes = []
-
-    def write(src, dst):
-        copy = pltpu.make_async_copy(src, dst, out_sem.at[len(writes)])
-        copy.start()
-        writes.append(copy)
 
     def settle():
         for copy in started:
@@ -217,8 +209,6 @@
             rb.at[z, y], rb.at[z, y], p1b_s.at[d], p1b_r.at[y], to * NZ + z, t
         )
 
-    write(v_lu, log_up)
-    write(v_ld, log_dn)
 
     for d in range(1, NY):
         src = at_y(d)
@@ -321,27 +311,17 @@
         cut = slice(h * HALF, (h + 1) * HALF)
         v_fu[:, cut] = gram[:WIDTH] + jnp.where(same, DAMPING * trace_up / FLAT, 0.0)
         v_fd[:, cut] = gram[WIDTH:] + jnp.where(same, DAMPING * trace_dn / FLAT, 0.0)
-        write(v_fu.at[:, cut], f_up.at[:, cut])
-        write(v_fd.at[:, cut], f_dn.at[:, cut])
 
     settle()
-    for copy in writes:
+
+
+def hand_over(*refs):
+    given, taken, sems = refs[0:4], refs[4:8], refs[8]
+    copies = [pltpu.make_async_copy(given[i], taken[i], sems.at[i]) for i in (2, 3, 0, 1)]
+    for copy in copies:
+        copy.start()
+    for copy in copies:
         copy.wait()
-
-
-def hand_over(*refs):
-    given, taken, held = refs[0:4], refs[4:8], refs[8:12]
-    sem_in, sem_out = refs[12:]
-    order = (2, 3, 0, 1)
-    ins = [pltpu.make_async_copy(given[i], held[i], sem_in.at[i]) for i in order]
-    outs = [pltpu.make_async_copy(held[i], taken[i], sem_out.at[i]) for i in order]
-    for copy in ins:
-        copy.start()
-    for copy, onward in zip(ins, outs, strict=True):
-        copy.wait()
-        onward.start()
-    for onward in outs:
-        onward.wait()
 
 
 def body(
@@ -365,7 +345,7 @@
         kernel,
         out_shape=out_shape,
         in_specs=[pl.BlockSpec(memory_space=pltpu.HBM)] * 8,
-        out_specs=[pl.BlockSpec(memory_space=pltpu.HBM)] * 4,
+        out_specs=[pl.BlockSpec(memory_space=pltpu.VMEM)] * 4,
         scratch_shapes=[pltpu.VMEM(a.shape, a.dtype) for a in operands]
         + [
             pltpu.VMEM((NT, LEN, 2 * WIDTH), f32),
@@ -379,12 +359,11 @@
             pltpu.VMEM((NZ, NY, 8, HALF), f32),
             pltpu.VMEM((NZ, NY, 8, HALF), f32),
         ]
-        + [pltpu.VMEM(shape, f32) for shape in shapes]
-        + [dma((6 + 2 * (len(CUTS) - 1),)), dma((6,))]
+        + [dma((6 + 2 * (len(CUTS) - 1),))]
         + [dma((8,))] * 14
         + [dma((64,))] * 2,
         compiler_params=pltpu.CompilerParams(
-            collective_id=0, has_side_effects=True, vmem_limit_bytes=63 * 1024 * 1024
+            collective_id=0, has_side_effects=True, vmem_limit_bytes=54912 * 1024
         ),
         cost_estimate=pl.CostEstimate(
             flops=2 * 256 * 64 * 9216, bytes_accessed=6 * 1024 * 1024, transcendentals=0
@@ -393,9 +372,10 @@
     return pl.pallas_call(
         hand_over,
         out_shape=out_shape,
-        in_specs=[pl.BlockSpec(memory_space=pltpu.HBM)] * 4,
+        in_specs=[pl.BlockSpec(memory_space=pltpu.VMEM)] * 4,
         out_specs=[pl.BlockSpec(memory_space=pltpu.HBM)] * 4,
-        scratch_shapes=[pltpu.VMEM(shape, f32) for shape in shapes] + [dma((4,))] * 2,
+        scratch_shapes=[dma((4,))],
+        compiler_params=pltpu.CompilerParams(vmem_limit_bytes=1024 * 1024),
     )(*results)
 
 

time: 42.5 us -> 40.8 us (0.960)
  Pallas kernels: 41.7 us -> 40 us
    pallas_call x1, Pallas kernels: 1.7 us -> 0.74 us  [body(): pl.pallas_call(hand_over, out_shape=out_shape, in_specs=[pl.BlockSpec(mem...]
    pallas_call x1, Pallas kernels: 40 us -> 39.3 us  [body(): pl.pallas_call(kernel, out_shape=out_shape, in_specs=[pl.BlockSpec(memory...]
where the time goes in v4:
time: 40.8 us; the launch traced here: 40.7 us
  Pallas kernels  40 us (98%)
  between operations  0.64 us (2%)
    pallas_call x1, Pallas kernels, body(): pl.pallas_call(kernel, out_shape=out_shape, in_specs=[pl.BlockSpec(memory...  39.3 us

profile of v4, /device:TPU:16, one launch (start us, length us, event | category | flops | bytes accessed | tf_op | source)
XLA Modules:
  0.0 40.7 jit_solution(3045583825113014581)
XLA Ops:
  0.6 39.3 %shard_map.111 = (f32[4,512]{1,0:T(4,128)S(1)}, f32[4,512]{1,0:T(4,128)S(1)}, f32[64,512]{1,0:T(8,128)S(1)}, f32[64,512]{1,0:T(8,128)S(1)}) custom-call(bf16[256,1024]{1,0:T(8,128)(2,1)} %ia.1, bf16[256,3584]{1,0:T(8,128)(2,1)} %ha.1, bf16[256,3584]{1,0:T(8,128)(2,1)} %ug.1, bf16[256,1024]{1,0:T(8,128)(2,1)} %og.1, bf16[64,1024]{1,0:T(8,128)(2,1)} %iu.1, ...), custom_call_target="tpu_custom_call" | custom-call | flops 301989888 | bytes 6291456 | tf_op jit(solution)/shard_map/pallas_call | solution.py:344
  39.9 0.7 %shard_map.112 = (f32[4,512]{1,0:T(4,128)}, f32[4,512]{1,0:T(4,128)}, f32[64,512]{1,0:T(8,128)}, f32[64,512]{1,0:T(8,128)}) custom-call(f32[4,512]{1,0:T(4,128)S(1)} %get-tuple-element.8.refs_0_, f32[4,512]{1,0:T(4,128)S(1)} %get-tuple-element.9.refs_1_, f32[64,512]{1,0:T(8,128)S(1)} %get-tuple-element.10.refs_2_, f32[64,512]{1,0:T(8,128)S(1)} %get-tuple-element.11.refs_3_), custom_call_target="tpu_custom_call" | custom-call | tf_op jit(solution)/shard_map/pallas_call | solution.py:372

commit v5 on v4

--- a/solution.py
+++ b/solution.py
@@ -138,7 +138,7 @@
         return slim, total
 
     def scatter(side):
-        for d in range(NT // 2):
+        for d in (2, 1, 3, 0):
             other = (x + d) % (NT // 2)
             m = side * (NT // 2) + other
             to = 2 * other + side

time: 40.8 us -> 40.8 us (level)
  no operation moved by 1% of the time
where the time goes in v5:
time: 40.8 us; the launch traced here: 40.7 us
  Pallas kernels  40.1 us (98%)
  between operations  0.64 us (2%)
    pallas_call x1, Pallas kernels, body(): pl.pallas_call(kernel, out_shape=out_shape, in_specs=[pl.BlockSpec(memory...  39.3 us

profile of v5, /device:TPU:16, one launch (start us, length us, event | category | flops | bytes accessed | tf_op | source)
XLA Modules:
  0.0 40.7 jit_solution(11951446375937635987)
XLA Ops:
  0.6 39.3 %shard_map.111 = (f32[4,512]{1,0:T(4,128)S(1)}, f32[4,512]{1,0:T(4,128)S(1)}, f32[64,512]{1,0:T(8,128)S(1)}, f32[64,512]{1,0:T(8,128)S(1)}) custom-call(bf16[256,1024]{1,0:T(8,128)(2,1)} %ia.1, bf16[256,3584]{1,0:T(8,128)(2,1)} %ha.1, bf16[256,3584]{1,0:T(8,128)(2,1)} %ug.1, bf16[256,1024]{1,0:T(8,128)(2,1)} %og.1, bf16[64,1024]{1,0:T(8,128)(2,1)} %iu.1, ...), custom_call_target="tpu_custom_call" | custom-call | flops 301989888 | bytes 6291456 | tf_op jit(solution)/shard_map/pallas_call | solution.py:344
  40.0 0.7 %shard_map.112 = (f32[4,512]{1,0:T(4,128)}, f32[4,512]{1,0:T(4,128)}, f32[64,512]{1,0:T(8,128)}, f32[64,512]{1,0:T(8,128)}) custom-call(f32[4,512]{1,0:T(4,128)S(1)} %get-tuple-element.8.refs_0_, f32[4,512]{1,0:T(4,128)S(1)} %get-tuple-element.9.refs_1_, f32[64,512]{1,0:T(8,128)S(1)} %get-tuple-element.10.refs_2_, f32[64,512]{1,0:T(8,128)S(1)} %get-tuple-element.11.refs_3_), custom_call_target="tpu_custom_call" | custom-call | tf_op jit(solution)/shard_map/pallas_call | solution.py:372
